TPU v7x, 512 devices: a whole 4x4x16 slice. The times are simulated.
512 devices in a mesh: ctx: 32 (over z, core), tp: 4 (over x), dp: 4 (over y).
Axes of the slice: x: 4, y: 4, z: 16, core: 2. Of those that a mesh axis runs over, the one named last changes fastest.
Arguments:
- attention_out: bfloat16 [8192, 4096], P('ctx', ('tp', 'dp')), may hold values from -6 to 6
- output_weight: bfloat16 [4096, 2048], P(('tp', 'dp')), may hold values from -0.09375 to 0.09375
- residual: bfloat16 [8192, 2048], P(('ctx', 'tp')), may hold values from -6 to 6
- norm_gain: float32 [2048], replicated, may hold values from 0.25 to 1.75
- routed_experts: int32 [8192, 8], P(('ctx', 'tp')), may hold values from 0 to 127, as said below
- route_weights: float32 [8192, 8], P(('ctx', 'tp')), may hold values from 0.05 to 1
- gate_weight: bfloat16 [128, 1024, 2048], P(('ctx', 'tp'), 'dp'), may hold values from -0.125 to 0.125
- up_weight: bfloat16 [128, 1024, 2048], P(('ctx', 'tp'), 'dp'), may hold values from -0.125 to 0.125
- down_weight: bfloat16 [128, 1024, 2048], P(('ctx', 'tp'), 'dp'), may hold values from -0.75 to 0.75
Outputs:
- layer_out: bfloat16 [8192, 2048], P(('ctx', 'tp', 'dp'))
Inputs may be any that keep to these rules, and one draw needn't show every extreme that they name: `routed_experts`: each row names 8 different experts. In each aligned block of 64 rows no expert is named by more than 8 rows, and one expert, the same for all blocks, is named by exactly 8 rows in every block.
All inputs are finite; a program needn't handle non-finite values.
Results may differ from a plain program's by a relative error of at most 0.009.
Values may be sent and summed in bfloat16 or wider, within the bound.
A program may use at most 64 MiB of HBM per device.

v0:
```python
import jax
import jax.numpy as jnp
from jax import lax
from jax.sharding import PartitionSpec as P

EPSILON = 1e-06
F32 = jnp.float32
BF16 = jnp.bfloat16


def on_device(
    attention_out,
    output_weight,
    residual,
    norm_gain,
    routed_experts,
    route_weights,
    gate_weight,
    up_weight,
    down_weight,
):
    rows, width = residual.shape
    top = routed_experts.shape[1]
    replicas = lax.axis_size("dp")
    quarter = rows // replicas
    replica = lax.axis_index("dp")
    experts = lax.axis_size("ctx") * lax.axis_size("tp")
    capacity = min(rows, 2 * rows * top // experts)
    share = capacity // replicas
    down_full = lax.all_gather(down_weight[0], "dp", axis=0, tiled=True)
    partial = jnp.dot(attention_out, output_weight, preferred_element_type=F32).astype(BF16)
    arrived = lax.all_to_all(
        partial.reshape(-1, quarter, width), ("tp", "dp"), split_axis=0, concat_axis=0, tiled=True
    )
    summed = jnp.sum(arrived.astype(F32), axis=0)
    own_residual = lax.dynamic_slice_in_dim(residual, replica * quarter, quarter, 0)
    own_state = own_residual.astype(F32) + summed
    square = jnp.mean(own_state * own_state, axis=-1, keepdims=True)
    own_normed = (own_state * lax.rsqrt(square + EPSILON) * norm_gain).astype(BF16)
    normed = lax.all_gather(own_normed, "dp", axis=0, tiled=True)
    flat_ids = routed_experts.reshape(-1)
    copies = flat_ids.shape[0]
    after = lax.broadcasted_iota(jnp.int32, (copies, copies), 0) > lax.broadcasted_iota(
        jnp.int32, (copies, copies), 1
    )
    before = jnp.sum(((flat_ids[:, None] == flat_ids[None, :]) & after).astype(jnp.int32), axis=1)
    local = before - replica * share
    wanted = jnp.where((local >= 0) & (local < share), flat_ids * share + local, -1)
    wanted = wanted.reshape(rows, top)
    slots = jnp.arange(experts * share, dtype=jnp.int32)
    match = wanted[:, :, None] == slots[None, None, :]
    pick = jnp.any(match, axis=1).astype(BF16)
    outgoing = lax.dot_general(pick, normed, (((0,), (0,)), ((), ())), preferred_element_type=F32)
    outgoing = outgoing.astype(BF16).reshape(experts, share, width)
    incoming = lax.all_to_all(outgoing, ("ctx", "tp"), split_axis=0, concat_axis=0, tiled=True)
    flat_rows = lax.all_gather(incoming.reshape(-1, width), "dp", axis=0, tiled=True)
    gate_act = lax.dot_general(
        flat_rows, gate_weight[0], (((1,), (1,)), ((), ())), preferred_element_type=F32
    )
    up_act = lax.dot_general(
        flat_rows, up_weight[0], (((1,), (1,)), ((), ())), preferred_element_type=F32
    )
    hidden = (jax.nn.silu(gate_act) * up_act).astype(BF16)
    hidden = lax.all_to_all(
        hidden.reshape(replicas, experts * share, -1), "dp", split_axis=0, concat_axis=0, tiled=True
    )
    hidden = jnp.moveaxis(hidden, 0, 1).reshape(experts * share, -1)
    result = jnp.dot(hidden, down_full, preferred_element_type=F32).astype(BF16)
    returned = lax.all_to_all(
        result.reshape(experts, share, width),
        ("ctx", "tp"),
        split_axis=0,
        concat_axis=0,
        tiled=True,
    ).reshape(experts * share, width)
    probs = route_weights / jnp.sum(route_weights, axis=1, keepdims=True)
    spread = jnp.sum(jnp.where(match, probs[:, :, None], 0.0), axis=1)
    high = spread.astype(BF16)
    low = (spread - high.astype(F32)).astype(BF16)
    mixed = jnp.dot(high, returned, preferred_element_type=F32) + jnp.dot(
        low, returned, preferred_element_type=F32
    )
    pieces = mixed.astype(BF16).reshape(replicas, quarter, width)
    pieces = lax.all_to_all(pieces, "dp", 0, 0, tiled=True)
    return (own_state + jnp.sum(pieces.astype(F32), axis=0)).astype(BF16)


def solution(mesh):
    in_specs = (
        P("ctx", ("tp", "dp")),
        P(("tp", "dp"), None),
        P(("ctx", "tp"), None),
        P(),
        P(("ctx", "tp"), None),
        P(("ctx", "tp"), None),
        P(("ctx", "tp"), "dp", None),
        P(("ctx", "tp"), "dp", None),
        P(("ctx", "tp"), "dp", None),
    )
    out_specs = P(("ctx", "tp", "dp"), None)
    return jax.shard_map(
        on_device, mesh=mesh, in_specs=in_specs, out_specs=out_specs, check_vma=False
    )
```

profile of v0, /device:TPU:1, one launch (start us, length us, event | category | flops | bytes accessed | tf_op | source)
XLA Modules:
  0.0 324.0 jit_solution(239269866060184144)
XLA Ops:
  6.5 1.2 copy-done
  7.8 2.3 convolution_convert_fusion
  10.1 7.6 %all-to-all-start = ((bf16[16,16,2048]{2,1,0:T(8,128)(2,1)}), bf16[16,16,2048]{2,1,0:T(8,128)(2,1)S(1)}, u32[]{:S(2)}, u32[]{:S(2)}) async-start(bf16[16,16,2048]{2,1,0:T(8,128)(2,1)} %bitcast), calls=%async_computation | async-start | bytes 2097152 | tf_op jit(solution)/shard_map/all_to_all | solution.py:32
  18.6 13.3 %all-to-all-done = bf16[16,16,2048]{2,1,0:T(8,128)(2,1)S(1)} async-done(((bf16[16,16,2048]{2,1,0:T(8,128)(2,1)}), bf16[16,16,2048]{2,1,0:T(8,128)(2,1)S(1)}, u32[]{:S(2)}, u32[]{:S(2)}) %all-to-all-start) | async-done | bytes 1048608 | tf_op jit(solution)/shard_map/all_to_all | solution.py:32
  32.3 9.4 %all_gather.9 = bf16[64,2048]{1,0:T(8,128)(2,1)S(1)} all-gather(bf16[16,2048]{1,0:T(8,128)(2,1)S(1)} %multiply_convert_fusion), channel_id=1, replica_groups=mesh['ctx'=32,'tp'=4,'dp'=4] {'dp'}, dimensions={0}, use_global_device_ids=true | all-gather | bytes 327680 | tf_op jit(solution)/shard_map/all_gather | solution.py:40
  41.7 0.5 convolution_convert_fusion.1
  42.2 0.7 reshape.52
  42.9 78.9 %all_to_all.25 = bf16[128,2,2048]{2,1,0:T(2,128)(2,1)S(1)} all-to-all(bf16[128,2,2048]{2,1,0:T(2,128)(2,1)S(1)} %reshape.52), channel_id=1, replica_groups=mesh['ctx'=32,'tp'=4,'dp'=4] {'ctx','tp'}, dimensions={0} | all-to-all | bytes 2097152 | tf_op jit(solution)/shard_map/all_to_all | solution.py:55
  121.8 1.3 reshape.53
  123.2 0.7 all-gather.6.cloned.1.call-update
  123.9 45.6 %all-gather.4.cloned.1.call-done = bf16[1024,2048]{1,0:T(8,128)(2,1)} async-done(((bf16[256,2048]{1,0:T(8,128)(2,1)}), bf16[1024,2048]{1,0:T(8,128)(2,1)}) %all-gather.4.cloned.1.call-update) | async-done | bytes 4194320 | tf_op jit(solution)/shard_map/all_gather | solution.py:56
  169.5 3.6 %fusion.8 = f32[1024,256]{1,0:T(8,128)S(1)} fusion(bf16[1024,2048]{1,0:T(8,128)(2,1)} %all-gather.4.cloned.1.call-done, bf16[1,256,2048]{2,1,0:T(8,128)(2,1)S(1)} %copy-done.6), kind=kOutput, calls=%fused_computation.11 | convolution fusion | flops 1073741824 | bytes 6291456 | tf_op jit(solution)/shard_map/dot_general | solution.py:57
  173.1 2.5 fusion.6
  175.7 1.0 copy.21
  176.7 3.5 %all-to-all-start.2 = ((bf16[4,256,256]{1,2,0:T(8,128)(2,1)}), bf16[4,256,256]{1,2,0:T(8,128)(2,1)S(1)}, u32[]{:S(2)}, u32[]{:S(2)}) async-start(bf16[4,256,256]{1,2,0:T(8,128)(2,1)} %copy.21), calls=%async_computation.2 | async-start | bytes 1048576 | tf_op jit(solution)/shard_map/all_to_all | solution.py:64
  180.1 47.8 %all-gather.6.cloned.1.call-done = bf16[1,1024,2048]{2,1,0:T(8,128)(2,1)} async-done(((bf16[1,256,2048]{2,1,0:T(8,128)(2,1)}), bf16[1,1024,2048]{2,1,0:T(8,128)(2,1)}) %all-gather.6.cloned.1.call-update) | async-done | bytes 4194320 | tf_op jit(solution)/shard_map/all_gather | solution.py:30
  228.0 3.5 %fusion.2 = bf16[256,2048]{1,0:T(8,128)(2,1)S(1)} fusion(bf16[256,1024]{0,1:T(8,128)(2,1)S(1)} %bitcast.27, bf16[1,1024,2048]{2,1,0:T(8,128)(2,1)} %all-gather.6.cloned.1.call-done), kind=kOutput, calls=%fused_computation.2 | convolution fusion | flops 1074266112 | bytes 5767168 | tf_op jit(solution)/shard_map/dot_general | solution.py:68
  231.4 1.5 reshape.56
  233.0 16.6 %all-to-all-start.3 = ((bf16[128,2,2048]{2,1,0:T(2,128)(2,1)}), bf16[128,2,2048]{2,1,0:T(2,128)(2,1)S(1)}, u32[]{:S(2)}, u32[]{:S(2)}) async-start(bf16[128,2,2048]{2,1,0:T(2,128)(2,1)} %reshape.56), calls=%async_computation.3 | async-start | bytes 2097152 | tf_op jit(solution)/shard_map/all_to_all | solution.py:69
  249.9 54.9 %all-to-all-done.3 = bf16[128,2,2048]{2,1,0:T(2,128)(2,1)S(1)} async-done(((bf16[128,2,2048]{2,1,0:T(2,128)(2,1)}), bf16[128,2,2048]{2,1,0:T(2,128)(2,1)S(1)}, u32[]{:S(2)}, u32[]{:S(2)}) %all-to-all-start.3) | async-done | bytes 1048608 | tf_op jit(solution)/shard_map/all_to_all | solution.py:69
  304.8 0.4 reshape.57
  305.6 0.3 fusion.5
  305.9 9.8 %all_to_all.26 = bf16[4,16,2048]{2,1,0:T(8,128)(2,1)S(1)} all-to-all(bf16[4,16,2048]{2,1,0:T(8,128)(2,1)S(1)} %bitcast.26), channel_id=1, replica_groups=mesh['ctx'=32,'tp'=4,'dp'=4] {'dp'}, dimensions={0} | all-to-all | bytes 524288 | tf_op jit(solution)/shard_map/all_to_all | solution.py:84
  315.7 1.5 add_convert_fusion
  (36 shorter events, 2.1 us)
Async XLA Ops:
  6.5 1.2 copy-start
  6.5 11.2 %copy-start.2 = (s32[64,8]{0,1:T(8,128)S(1)}, s32[64,8]{0,1:T(8,128)}, u32[]{:S(2)}) copy-start(s32[64,8]{0,1:T(8,128)} %param.13) | copy-start | bytes 6148
  6.5 25.5 %copy-start.1 = (bf16[64,2048]{1,0:T(8,128)(2,1)S(1)}, bf16[64,2048]{1,0:T(8,128)(2,1)}, u32[]{:S(2)}) copy-start(bf16[64,2048]{1,0:T(8,128)(2,1)} %param.11) | copy-start | bytes 786436
  6.5 25.7 %copy-start.4 = (f32[2048]{0:T(1024)S(1)}, f32[2048]{0:T(1024)}, u32[]{:S(2)}) copy-start(f32[2048]{0:T(1024)} %param.12) | copy-start | bytes 24580
  10.1 21.8 %all-to-all-start = ((bf16[16,16,2048]{2,1,0:T(8,128)(2,1)}), bf16[16,16,2048]{2,1,0:T(8,128)(2,1)S(1)}, u32[]{:S(2)}, u32[]{:S(2)}) async-start(bf16[16,16,2048]{2,1,0:T(8,128)(2,1)} %bitcast), calls=%async_computation | async-start | bytes 2097152 | tf_op jit(solution)/shard_map/all_to_all | solution.py:32
  17.7 151.8 %all-gather.4.cloned.1.call-start = ((), (), s32[]{:S(2)}) async-start(), calls=%async_computation.5 | async-start | bytes 5242880 | tf_op jit(solution)/shard_map/all_gather | solution.py:56
  121.8 47.7 %copy-start.6 = (bf16[1,256,2048]{2,1,0:T(8,128)(2,1)S(1)}, bf16[1,256,2048]{2,1,0:T(8,128)(2,1)}, u32[]{:S(2)}) copy-start(bf16[1,256,2048]{2,1,0:T(8,128)(2,1)} %param.15) | copy-start | bytes 3145732
  123.1 104.9 %all-gather.6.cloned.1.call-start = ((), (), s32[]{:S(2)}) async-start(), calls=%async_computation.6 | async-start | bytes 5242880 | tf_op jit(solution)/shard_map/all_gather | solution.py:30
  169.5 3.6 %copy-start.5 = (bf16[1024,2048]{1,0:T(8,128)(2,1)S(1)}, bf16[1024,2048]{1,0:T(8,128)(2,1)}, u32[]{:S(2)}) copy-start(bf16[1024,2048]{1,0:T(8,128)(2,1)} %all-gather.4.cloned.1.call-done) | copy-start | bytes 12582916
  176.7 51.3 %all-to-all-start.2 = ((bf16[4,256,256]{1,2,0:T(8,128)(2,1)}), bf16[4,256,256]{1,2,0:T(8,128)(2,1)S(1)}, u32[]{:S(2)}, u32[]{:S(2)}) async-start(bf16[4,256,256]{1,2,0:T(8,128)(2,1)} %copy.21), calls=%async_computation.2 | async-start | bytes 1048576 | tf_op jit(solution)/shard_map/all_to_all | solution.py:64
  228.0 21.6 %copy-start.3 = (f32[64,8]{0,1:T(8,128)S(1)}, f32[64,8]{0,1:T(8,128)}, u32[]{:S(2)}) copy-start(f32[64,8]{0,1:T(8,128)} %param.14) | copy-start | bytes 6148
  233.0 71.9 %all-to-all-start.3 = ((bf16[128,2,2048]{2,1,0:T(2,128)(2,1)}), bf16[128,2,2048]{2,1,0:T(2,128)(2,1)S(1)}, u32[]{:S(2)}, u32[]{:S(2)}) async-start(bf16[128,2,2048]{2,1,0:T(2,128)(2,1)} %reshape.56), calls=%async_computation.3 | async-start | bytes 2097152 | tf_op jit(solution)/shard_map/all_to_all | solution.py:69
Sparse Core Ops, SparseCore 0:
  123.2 46.1 all-gather.3
  171.6 56.3 all-gather.5
where the time goes:
time: 325 us; the launch traced here: 324 us
  waiting for transfers between devices  162 us (50%)
  blocking collectives  98 us (30%)
  starting transfers between devices  27.7 us (9%)
  between operations  13.6 us (4%)
  matrix products  13 us (4%)
  local copies, waits for them, and re-layouts  6.6 us (2%)
    all_to_all x1, blocking collectives, on_device(): lax.all_to_all(outgoing, ('ctx', 'tp'), split_axis=0, concat_axis=0, tile...  78.9 us
    all_to_all x1, waiting for transfers between devices, on_device(): lax.all_to_all(result.reshape(experts, share, width), ('ctx', 'tp'), spli...  54.9 us
    all_gather x1, waiting for transfers between devices, on_device(): down_full = lax.all_gather(down_weight[0], 'dp', axis=0, tiled=True)  47.8 us
    all_gather x1, waiting for transfers between devices, on_device(): lax.all_gather(incoming.reshape(-1, width), 'dp', axis=0, tiled=True)  45.6 us
    all_to_all x1, starting transfers between devices, on_device(): lax.all_to_all(result.reshape(experts, share, width), ('ctx', 'tp'), spli...  16.6 us
    all_to_all x1, waiting for transfers between devices, on_device(): lax.all_to_all(partial.reshape(-1, quarter, width), ('tp', 'dp'), split_a...  13.3 us
    all_to_all x1, blocking collectives, on_device(): pieces = lax.all_to_all(pieces, 'dp', 0, 0, tiled=True)  9.77 us
    all_gather x1, blocking collectives, on_device(): normed = lax.all_gather(own_normed, 'dp', axis=0, tiled=True)  9.37 us
  transfers between devices with their start and end apart: 5, of which 4 were waited for; matrix products, arithmetic and copies ran while one was open for 3% of the time, Pallas kernels for 0%

commit v1 on v0

--- a/solution.py
+++ b/solution.py
@@ -27,7 +27,12 @@
     experts = lax.axis_size("ctx") * lax.axis_size("tp")
     capacity = min(rows, 2 * rows * top // experts)
     share = capacity // replicas
-    down_full = lax.all_gather(down_weight[0], "dp", axis=0, tiled=True)
+    ring = [down_weight[0]]
+    for hop in range(3):
+        ring.append(lax.ppermute(ring[-1], "dp", [(dev, (dev + 1) % 4) for dev in range(4)]))
+    down_full = jnp.roll(
+        jnp.concatenate(ring[::-1], axis=0), (lax.axis_index("dp") + 1) * ring[0].shape[0], axis=0
+    )
     partial = jnp.dot(attention_out, output_weight, preferred_element_type=F32).astype(BF16)
     arrived = lax.all_to_all(
         partial.reshape(-1, quarter, width), ("tp", "dp"), split_axis=0, concat_axis=0, tiled=True

time: 325 us -> 359 us (1.10)
  waiting for transfers between devices: 162 us -> 179 us
  local copies, waits for them, and re-layouts: 6.6 us -> 21.8 us
    ppermute x0 -> x3, waiting for transfers between devices: none -> 106 us  [on_device(): lax.ppermute(ring[-1], 'dp', [(dev, (dev + 1) % 4) for dev in range(4)])]
    all_gather x1 -> x0, waiting for transfers between devices: 47.8 us -> none  [on_device(): down_full = lax.all_gather(down_weight[0], 'dp', axis=0, tiled=True)]
    all_gather x1, waiting for transfers between devices: 45.6 us -> 0.01 us  [on_device(): lax.all_gather(incoming.reshape(-1, width), 'dp', axis=0, tiled=True)]
    unnamed x15 -> x14, local copies, waits for them, and re-layouts: 1.33 us -> 14.6 us
    all_to_all x1, starting transfers between devices: 16.6 us -> 8.81 us  [on_device(): lax.all_to_all(result.reshape(experts, share, width), ('ctx', 'tp'), spli...]
    all_to_all x1, waiting for transfers between devices: 0.01 us -> 6.56 us  [on_device(): lax.all_to_all(hidden.reshape(replicas, experts * share, -1), 'dp', split...]
    ppermute x0 -> x3, starting transfers between devices: none -> 5.74 us  [on_device(): lax.ppermute(ring[-1], 'dp', [(dev, (dev + 1) % 4) for dev in range(4)])]
  transfers between devices with their start and end apart: 5 -> 7, of which waited for: 4 -> 6; matrix products, arithmetic and copies ran while one was open for 3% -> 5% of each run, Pallas kernels for 0% -> 0%
where the time goes in v1:
time: 359 us; the launch traced here: 358 us
  waiting for transfers between devices  179 us (50%)
  blocking collectives  98.1 us (27%)
  starting transfers between devices  25.6 us (7%)
  local copies, waits for them, and re-layouts  21.8 us (6%)
  matrix products  14.4 us (4%)
  between operations  13.6 us (4%)
  other arithmetic  5.07 us (1%)
    ppermute x3, waiting for transfers between devices, on_device(): lax.ppermute(ring[-1], 'dp', [(dev, (dev + 1) % 4) for dev in range(4)])  106 us
    all_to_all x1, blocking collectives, on_device(): lax.all_to_all(outgoing, ('ctx', 'tp'), split_axis=0, concat_axis=0, tile...  79.1 us
    all_to_all x1, waiting for transfers between devices, on_device(): lax.all_to_all(result.reshape(experts, share, width), ('ctx', 'tp'), spli...  54.9 us
    unnamed x14, local copies, waits for them, and re-layouts  14.6 us
    all_to_all x1, waiting for transfers between devices, on_device(): lax.all_to_all(partial.reshape(-1, quarter, width), ('tp', 'dp'), split_a...  11.9 us
    all_to_all x1, blocking collectives, on_device(): pieces = lax.all_to_all(pieces, 'dp', 0, 0, tiled=True)  9.59 us
    all_gather x1, blocking collectives, on_device(): normed = lax.all_gather(own_normed, 'dp', axis=0, tiled=True)  9.37 us
    all_to_all x1, starting transfers between devices, on_device(): lax.all_to_all(result.reshape(experts, share, width), ('ctx', 'tp'), spli...  8.81 us
  transfers between devices with their start and end apart: 7, of which 6 were waited for; matrix products, arithmetic and copies ran while one was open for 5% of the time, Pallas kernels for 0%

profile of v1, /device:TPU:1, one launch (start us, length us, event | category | flops | bytes accessed | tf_op | source)
XLA Modules:
  0.0 357.9 jit_solution(14574179313721220625)
XLA Ops:
  7.8 2.3 convolution_convert_fusion
  10.1 7.6 %all-to-all-start = ((bf16[16,16,2048]{2,1,0:T(8,128)(2,1)}), bf16[16,16,2048]{2,1,0:T(8,128)(2,1)S(1)}, u32[]{:S(2)}, u32[]{:S(2)}) async-start(bf16[16,16,2048]{2,1,0:T(8,128)(2,1)} %bitcast.25), calls=%async_computation | async-start | bytes 2097152 | tf_op jit(solution)/shard_map/all_to_all | solution.py:37
  20.0 11.9 %all-to-all-done = bf16[16,16,2048]{2,1,0:T(8,128)(2,1)S(1)} async-done(((bf16[16,16,2048]{2,1,0:T(8,128)(2,1)}), bf16[16,16,2048]{2,1,0:T(8,128)(2,1)S(1)}, u32[]{:S(2)}, u32[]{:S(2)}) %all-to-all-start) | async-done | bytes 1048608 | tf_op jit(solution)/shard_map/all_to_all | solution.py:37
  34.0 9.4 %all_gather.6 = bf16[64,2048]{1,0:T(8,128)(2,1)S(1)} all-gather(bf16[16,2048]{1,0:T(8,128)(2,1)S(1)} %multiply_convert_fusion), channel_id=1, replica_groups=mesh['ctx'=32,'tp'=4,'dp'=4] {'dp'}, dimensions={0}, use_global_device_ids=true | all-gather | bytes 327680 | tf_op jit(solution)/shard_map/all_gather | solution.py:45
  43.9 1.5 reshape.52
  45.4 79.1 %all_to_all.25 = bf16[128,2,2048]{2,1,0:T(2,128)(2,1)S(1)} all-to-all(bf16[128,2,2048]{2,1,0:T(2,128)(2,1)} %reshape.52), channel_id=1, replica_groups=mesh['ctx'=32,'tp'=4,'dp'=4] {'ctx','tp'}, dimensions={0} | all-to-all | bytes 2097152 | tf_op jit(solution)/shard_map/all_to_all | solution.py:60
  125.8 1.9 collective-permute-start
  127.7 42.0 %collective-permute-done = bf16[256,2048]{1,0:T(8,128)(2,1)S(1)} collective-permute-done((bf16[256,2048]{1,0:T(8,128)(2,1)S(1)}, bf16[256,2048]{1,0:T(8,128)(2,1)S(1)}, u32[]{:S(2)}, u32[]{:S(2)}) %collective-permute-start) | collective-permute-done | bytes 1048608 | tf_op jit(solution)/shard_map/ppermute | solution.py:32
  169.7 1.9 collective-permute-start.1
  171.6 38.4 %collective-permute-done.1 = bf16[256,2048]{1,0:T(8,128)(2,1)} collective-permute-done((bf16[256,2048]{1,0:T(8,128)(2,1)S(1)}, bf16[256,2048]{1,0:T(8,128)(2,1)}, u32[]{:S(2)}, u32[]{:S(2)}) %collective-permute-start.1) | collective-permute-done | bytes 1048608 | tf_op jit(solution)/shard_map/ppermute | solution.py:32
  210.0 1.9 collective-permute-start.2
  212.0 25.5 %collective-permute-done.2 = bf16[256,2048]{1,0:T(8,128)(2,1)} collective-permute-done((bf16[256,2048]{1,0:T(8,128)(2,1)}, bf16[256,2048]{1,0:T(8,128)(2,1)}, u32[]{:S(2)}, u32[]{:S(2)}) %collective-permute-start.2) | collective-permute-done | bytes 1048608 | tf_op jit(solution)/shard_map/ppermute | solution.py:32
  237.5 2.3 constant_dynamic-update-slice_fusion.7
  239.8 2.4 constant_dynamic-update-slice_fusion.6
  244.3 2.3 constant_dynamic-update-slice_fusion.3
  246.6 2.4 constant_dynamic-update-slice_fusion.2
  250.1 3.8 %fusion.8 = f32[1024,256]{1,0:T(8,128)S(1)} fusion(bf16[1024,2048]{1,0:T(8,128)(2,1)} %all-gather.2.cloned.1.call-done, bf16[1,256,2048]{2,1,0:T(8,128)(2,1)} %param.15), kind=kOutput, calls=%fused_computation.11 | convolution fusion | flops 1073741824 | bytes 6291456 | tf_op jit(solution)/shard_map/dot_general | solution.py:62
  253.8 3.8 %fusion.6 = bf16[1024,256]{1,0:T(8,128)(2,1)S(1)} fusion(bf16[1024,2048]{1,0:T(8,128)(2,1)} %all-gather.2.cloned.1.call-done, bf16[1,256,2048]{2,1,0:T(8,128)(2,1)} %param.16, f32[1024,256]{1,0:T(8,128)S(1)} %fusion.8), kind=kOutput, calls=%fused_computation.9 | convolution fusion | flops 1075314688 | bytes 6815744 | tf_op jit(solution)/shard_map/dot_general | solution.py:65
  258.7 3.5 all-to-all-start.2
  263.3 6.6 %all-to-all-done.2 = bf16[4,256,256]{1,2,0:T(8,128)(2,1)S(1)} async-done(((bf16[4,256,256]{1,2,0:T(8,128)(2,1)}), bf16[4,256,256]{1,2,0:T(8,128)(2,1)S(1)}, u32[]{:S(2)}, u32[]{:S(2)}) %all-to-all-start.2) | async-done | bytes 524320 | tf_op jit(solution)/shard_map/all_to_all | solution.py:69
  269.8 3.5 fusion.2
  274.8 8.8 %all-to-all-start.3 = ((bf16[128,2,2048]{2,1,0:T(2,128)(2,1)}), bf16[128,2,2048]{2,1,0:T(2,128)(2,1)S(1)}, u32[]{:S(2)}, u32[]{:S(2)}) async-start(bf16[128,2,2048]{2,1,0:T(2,128)(2,1)} %reshape.56), calls=%async_computation.3 | async-start | bytes 2097152 | tf_op jit(solution)/shard_map/all_to_all | solution.py:74
  284.0 54.9 %all-to-all-done.3 = bf16[128,2,2048]{2,1,0:T(2,128)(2,1)S(1)} async-done(((bf16[128,2,2048]{2,1,0:T(2,128)(2,1)}), bf16[128,2,2048]{2,1,0:T(2,128)(2,1)S(1)}, u32[]{:S(2)}, u32[]{:S(2)}) %all-to-all-start.3) | async-done | bytes 1048608 | tf_op jit(solution)/shard_map/all_to_all | solution.py:74
  339.9 9.6 %all_to_all.26 = bf16[4,16,2048]{2,1,0:T(8,128)(2,1)S(1)} all-to-all(bf16[4,16,2048]{2,1,0:T(8,128)(2,1)S(1)} %bitcast.26), channel_id=1, replica_groups=mesh['ctx'=32,'tp'=4,'dp'=4] {'dp'}, dimensions={0} | all-to-all | bytes 524288 | tf_op jit(solution)/shard_map/all_to_all | solution.py:89
  (39 shorter events, 17.1 us)
Async XLA Ops:
  6.5 1.2 copy-start
  6.5 119.2 %copy-start.1 = (bf16[1,256,2048]{2,1,0:T(8,128)(2,1)S(1)}, bf16[1,256,2048]{2,1,0:T(8,128)(2,1)}, u32[]{:S(2)}) copy-start(bf16[1,256,2048]{2,1,0:T(8,128)(2,1)} %param.17) | copy-start | bytes 3145732
  10.1 21.8 %all-to-all-start = ((bf16[16,16,2048]{2,1,0:T(8,128)(2,1)}), bf16[16,16,2048]{2,1,0:T(8,128)(2,1)S(1)}, u32[]{:S(2)}, u32[]{:S(2)}) async-start(bf16[16,16,2048]{2,1,0:T(8,128)(2,1)} %bitcast.25), calls=%async_computation | async-start | bytes 2097152 | tf_op jit(solution)/shard_map/all_to_all | solution.py:37
  17.7 232.4 %all-gather.2.cloned.1.call-start = ((), (), s32[]{:S(2)}) async-start(), calls=%async_computation.5 | async-start | bytes 5242880 | tf_op jit(solution)/shard_map/all_gather | solution.py:61
  125.8 44.0 %collective-permute-start = (bf16[256,2048]{1,0:T(8,128)(2,1)S(1)}, bf16[256,2048]{1,0:T(8,128)(2,1)S(1)}, u32[]{:S(2)}, u32[]{:S(2)}) collective-permute-start(bf16[256,2048]{1,0:T(8,128)(2,1)S(1)} %bitcast.24), channel_id=1, source_target_pairs={{0,1},{1,2},{2,3},{3,0},{4,5},{5,6},{6,7},{7,4},{8,9},{9,10},{10,1... | collective-permute-start | bytes 3145736 | tf_op jit(solution)/shard_map/ppermute | solution.py:32
  169.7 40.3 %collective-permute-start.1 = (bf16[256,2048]{1,0:T(8,128)(2,1)S(1)}, bf16[256,2048]{1,0:T(8,128)(2,1)}, u32[]{:S(2)}, u32[]{:S(2)}) collective-permute-start(bf16[256,2048]{1,0:T(8,128)(2,1)S(1)} %collective-permute-done), channel_id=1, source_target_pairs={{0,1},{1,2},{2,3},{3,0},{4,5},{5,6},{6,7},{7,4},{8,9},{9,10},{10,1... | collective-permute-start | bytes 3145736 | tf_op jit(solution)/shard_map/ppermute | solution.py:32
  210.0 27.4 %collective-permute-start.2 = (bf16[256,2048]{1,0:T(8,128)(2,1)}, bf16[256,2048]{1,0:T(8,128)(2,1)}, u32[]{:S(2)}, u32[]{:S(2)}) collective-permute-start(bf16[256,2048]{1,0:T(8,128)(2,1)} %collective-permute-done.1), channel_id=1, source_target_pairs={{0,1},{1,2},{2,3},{3,0},{4,5},{5,6},{6,7},{7,4},{8,9},{9,10},{10,1... | collective-permute-start | bytes 3145736 | tf_op jit(solution)/shard_map/ppermute | solution.py:32
  257.7 26.0 %copy-start.2 = (f32[64,8]{0,1:T(8,128)S(1)}, f32[64,8]{0,1:T(8,128)}, u32[]{:S(2)}) copy-start(f32[64,8]{0,1:T(8,128)} %param.14) | copy-start | bytes 6148
  258.7 11.1 %all-to-all-start.2 = ((bf16[4,256,256]{1,2,0:T(8,128)(2,1)}), bf16[4,256,256]{1,2,0:T(8,128)(2,1)S(1)}, u32[]{:S(2)}, u32[]{:S(2)}) async-start(bf16[4,256,256]{1,2,0:T(8,128)(2,1)} %copy.21), calls=%async_computation.2 | async-start | bytes 1048576 | tf_op jit(solution)/shard_map/all_to_all | solution.py:69
  274.8 64.1 %all-to-all-start.3 = ((bf16[128,2,2048]{2,1,0:T(2,128)(2,1)}), bf16[128,2,2048]{2,1,0:T(2,128)(2,1)S(1)}, u32[]{:S(2)}, u32[]{:S(2)}) async-start(bf16[128,2,2048]{2,1,0:T(2,128)(2,1)} %reshape.56), calls=%async_computation.3 | async-start | bytes 2097152 | tf_op jit(solution)/shard_map/all_to_all | solution.py:74
Sparse Core Ops, SparseCore 0:
  125.9 74.1 all-gather.1
